TPU v7x, 128 devices: a whole 4x4x4 slice. The times are simulated.
128 devices in a mesh: lat: 8 (over x_hi, y), lon: 16 (over x_lo, z, core).
Axes of the slice: x: 4 (x_hi: 2, x_lo: 2; x = x_hi * 2 + x_lo), y: 4, z: 4, core: 2. Of those that a mesh axis runs over, the one named last changes fastest.
Arguments:
- tokens: bfloat16 [3, 96, 384, 512], P(None, 'lat', 'lon'), may hold values from -6 to 6
- region_ids: int32 [96, 384], replicated, may hold values from 0 to 15, as said below
- w_qkv: bfloat16 [2, 512, 1536], replicated, may hold values from -0.30935922 to 0.30935922
- w_proj: bfloat16 [2, 512, 512], replicated, may hold values from -0.25 to 0.25
- w_up: bfloat16 [2, 512, 2048], replicated, may hold values from -0.25 to 0.25
- w_down: bfloat16 [2, 2048, 512], replicated, may hold values from -0.125 to 0.125
- merge_first: bfloat16 [2048, 1024], replicated, may hold values from -0.125 to 0.125
- merge_second: bfloat16 [4096, 2048], P(None, 'lon'), may hold values from -0.09375 to 0.09375
Outputs:
- fine: bfloat16 [3, 96, 384, 512], P(None, 'lat', 'lon')
- coarse: bfloat16 [3, 24, 96, 2048], P(None, 'lat', 'lon')
Inputs may be any that keep to these rules, and one draw needn't show every extreme that they name: `region_ids`: regions are rectangles: latitude rows fall into contiguous bands and longitude columns into contiguous bands, and a cell's id is 4 times its latitude band's number modulo 4 plus its longitude band's number modulo 4. A band begins only at row or column 0 or at an index that is not a multiple of 3.
All inputs are finite; a program needn't handle non-finite values.
Results may differ from a plain program's by a relative error of at most 0.025.
Values may be sent and summed in bfloat16 or wider, within the bound.
A program may use at most 192 MiB of HBM per device.

v0:
```python
import functools

import jax
import jax.numpy as jnp
import numpy as np
from jax import lax
from jax.experimental import pallas as pl
from jax.experimental.pallas import tpu as pltpu
from jax.sharding import PartitionSpec as P

MESH = pl.DeviceIdType.MESH
BF = jnp.bfloat16
F32 = jnp.float32
EPS = 1e-05
D = 512
FF = 2048
CELL = 64
WIN = 4 * CELL
SCORE_SCALE = 0.125 * 1.4426950408889634
NEG = -1e30

ERF_P = 0.3275911 * 0.7071067811865476
ERF_A = tuple(0.5 * a for a in (0.254829592, -0.284496736, 1.421413741, -1.453152027, 1.061405429))


def tables():
    out_of = np.zeros((432, 512), np.float32)
    for level in range(3):
        for row in range(6):
            for col in range(24):
                cell = (row // 3) * 4 + col // 6
                within = level * 18 + (row % 3) * 6 + col % 6
                out_of[level * 144 + row * 24 + col, cell * CELL + within] = 1
    quads = np.zeros((4 * 256, 16 * CELL), np.float32)
    for q1 in range(4):
        for q2 in range(4):
            for level in range(3):
                for i2 in range(3):
                    for j2 in range(6):
                        i, j = 2 * i2 + q2 % 2, 2 * j2 + q2 // 2
                        row, col = 2 * i + q1 % 2, 2 * j + q1 // 2
                        cell = (row // 3) * 4 + col // 6
                        within = level * 18 + (row % 3) * 6 + col % 6
                        quads[q1 * 256 + q2 * 64 + level * 18 + i2 * 6 + j2, cell * CELL + within] = 1
    place = np.zeros((4 * WIN, 256), np.float32)
    for w in range(4):
        for cell in range(4):
            for within in range(CELL):
                t = w * WIN + cell * CELL + within
                if within >= 54:
                    place[t, 15] = 1
                    place[t, 128] = 1
                else:
                    row = 6 * (w // 2) + 3 * (cell // 2) + (within // 6) % 3
                    col = 12 * (w % 2) + 6 * (cell % 2) + within % 6
                    place[t, row] = 1
                    place[t, 128 + col] = 1
    return out_of, quads, place


def dot(a, b):
    return jnp.dot(a, b, preferred_element_type=F32)


def dot_nt(a, b):
    return lax.dot_general(a, b, (((1,), (1,)), ((), ())), preferred_element_type=F32)


def layer_norm(v):
    center = v - jnp.mean(v, axis=-1, keepdims=True)
    spread = jnp.mean(center * center, axis=-1, keepdims=True)
    return center * lax.rsqrt(spread + EPS)


def gelu(u):
    size = jnp.abs(u)
    t = pl.reciprocal(1.0 + ERF_P * size, approx=True)
    a1, a2, a3, a4, a5 = ERF_A
    poly = t * (a1 + t * (a2 + t * (a3 + t * (a4 + t * a5))))
    tail = size * (poly * jnp.exp2(u * u * (-0.5 * 1.4426950408889634)))
    return jnp.maximum(u, 0.0) - tail


def window_block(cells, r, c, l, bias, b, wqkv, wproj, wup, wdown, qkv, att, mid, acc):
    x = cells[pl.ds(r, 2), pl.ds(c, 2)].reshape(WIN, D).astype(F32)
    normed = layer_norm(x).astype(BF)
    for k in range(3):
        cols = slice(k * 512, (k + 1) * 512)
        qkv[:, cols] = dot(normed, wqkv[l, :, cols]).astype(BF)
    low = lax.broadcasted_iota(jnp.int32, (WIN, 128), 1) < 64
    ones = jnp.ones((WIN, 128), BF)
    zero = jnp.zeros((WIN, 128), BF)
    for pair in range(4):
        q = qkv[:, pair * 128 : (pair + 1) * 128]
        k = qkv[:, 512 + pair * 128 : 512 + (pair + 1) * 128]
        v = jnp.concatenate([qkv[:, 1024 + pair * 128 : 1024 + (pair + 1) * 128], ones], axis=1)
        outs = []
        for part in range(2):
            qm = jnp.where(low, q, zero) if part == 0 else jnp.where(low, zero, q)
            s = dot_nt(qm, k) + bias[b]
            m = jnp.max(s, axis=-1, keepdims=True)
            p = jnp.exp2((s - m) * SCORE_SCALE).astype(BF)
            o = dot(p, v)
            outs.append(o[:, :128] * pl.reciprocal(o[:, 128:], approx=False))
        att[:, pair * 128 : (pair + 1) * 128] = jnp.where(low, outs[0], outs[1]).astype(BF)
    middle = (x + dot(att[...], wproj[l])).astype(BF).astype(F32)
    acc[...] = middle
    mid[...] = layer_norm(middle).astype(BF)
    for k in range(4):
        cols = slice(k * 512, (k + 1) * 512)
        hidden = gelu(dot(mid[...], wup[l, :, cols])).astype(BF)
        acc[...] += dot(hidden, wdown[l, cols, :])
    cells[pl.ds(r, 2), pl.ds(c, 2)] = acc[...].astype(BF).reshape(2, 2, CELL, D)


def kernel(
    tok_h, ids_h, wqkv_h, wproj_h, wup_h, wdown_h, wm1_h, wm2_h, pin_h, pout_h, quads_h, place_h,
    fine_o, coarse_o,
    tok, ids, wqkv, wproj, wup, wdown, wm1, w2, pin, pout, quads, place,
    cells, ret, bias, qkv, att, mid, acc, nq, rows, cown, cgive, cret, fine_s, coarse_s,
    lsem, osem, hsend, hrecv, wsend, wrecv,
):
    lat, lon = lax.axis_index("lat"), lax.axis_index("lon")
    xh, xl = lax.div(lat, 4), lax.div(lon, 8)
    z, core = lax.rem(lax.div(lon, 2), 4), lax.rem(lon, 2)
    lat_up, lat_dn = lax.rem(lat + 1, 8), lax.rem(lat + 7, 8)
    lon_up, lon_dn = lax.rem(lon + 1, 16), lax.rem(lon + 15, 16)
    z_up, z_dn, z_far = lax.rem(z + 1, 4), lax.rem(z + 3, 4), lax.rem(z + 2, 4)
    above, below = (lat, xl * 8 + z_up * 2 + core), (lat, xl * 8 + z_dn * 2 + core)
    side_a = (lat, (1 - xl) * 8 + z * 2 + core)
    side_b = (lax.rem(lat + 4, 8), (1 - xl) * 8 + z * 2 + core)
    twin = (lat, xl * 8 + z * 2 + 1 - core)
    partners = (
        (lat_up, lon), (lat_dn, lon), (lat, lon_up), (lat, lon_dn), (lat_up, lon_up), (lat_dn, lon_dn),
        above, below, side_a, side_b, twin,
    )
    barrier = pltpu.get_barrier_semaphore()
    for device in partners:
        pl.semaphore_signal(barrier, inc=1, device_id=device, device_id_type=MESH)

    mine = xl * 4 + z
    loads = [
        (tok_h, tok), (pin_h, pin), (ids_h, ids), (place_h, place),
        (wqkv_h.at[0], wqkv.at[0]), (wproj_h.at[0], wproj.at[0]), (wup_h.at[0], wup.at[0]), (wdown_h.at[0], wdown.at[0]),
        (wqkv_h.at[1], wqkv.at[1]), (wproj_h.at[1], wproj.at[1]), (wup_h.at[1], wup.at[1]), (wdown_h.at[1], wdown.at[1]),
        (pout_h, pout), (quads_h, quads), (wm1_h, wm1), (wm2_h, w2.at[mine]),
    ]
    loads = [pltpu.make_async_copy(src, dst, lsem.at[i]) for i, (src, dst) in enumerate(loads)]
    for load in loads:
        load.start()

    def halo(i, src, dst, device):
        return pltpu.make_async_remote_copy(
            src_ref=src, dst_ref=dst, send_sem=hsend.at[i], recv_sem=hrecv.at[i], device_id=device, device_id_type=MESH
        )

    def give(i, src, dst, device):
        return pltpu.make_async_remote_copy(
            src_ref=src, dst_ref=dst, send_sem=wsend.at[i], recv_sem=wrecv.at[i], device_id=device, device_id_type=MESH
        )

    half = (pl.ds(0, 2048), pl.ds(2048, 2048))
    s_dn, s_up, s_far = xl * 4 + z_dn, xl * 4 + z_up, xl * 4 + z_far
    weights = [
        give(0, wm2_h, w2.at[mine], above),
        give(1, wm2_h, w2.at[mine], below),
        give(2, wm2_h.at[half[0]], w2.at[mine, half[0]], side_a),
        give(3, wm2_h.at[half[1]], w2.at[mine, half[1]], side_b),
        give(4, w2.at[s_dn, half[0]], w2.at[s_dn, half[0]], above),
        give(5, w2.at[s_up, half[1]], w2.at[s_up, half[1]], below),
        give(6, w2.at[s_dn, half[0]], w2.at[s_dn, half[0]], side_a),
        give(7, w2.at[s_dn, half[1]], w2.at[s_dn, half[1]], side_b),
        give(8, w2.at[s_up, half[0]], w2.at[s_up, half[0]], side_a),
        give(9, w2.at[s_up, half[1]], w2.at[s_up, half[1]], side_b),
        give(10, w2.at[s_far, half[0]], w2.at[s_far, half[0]], side_a),
        give(11, w2.at[s_far, half[1]], w2.at[s_far, half[1]], side_b),
        give(12, rows.at[0], rows.at[1], twin),
        give(13, cgive, cret, twin),
    ]
    out1 = [
        halo(0, cells.at[0, 0], cells.at[4, 4], (lat_dn, lon_dn)),
        halo(1, cells.at[0, 1], cells.at[4, 1], (lat_dn, lon)),
        halo(2, cells.at[1, 0], cells.at[1, 4], (lat, lon_dn)),
        halo(3, cells.at[0, pl.ds(2, 2)], cells.at[4, pl.ds(2, 2)], (lat_dn, lon)),
        halo(4, cells.at[pl.ds(2, 2), 0], cells.at[pl.ds(2, 2), 4], (lat, lon_dn)),
    ]
    out2 = [
        halo(5, cells.at[4, 4], ret.at[0], (lat_up, lon_up)),
        halo(6, cells.at[4, 3], ret.at[3], (lat_up, lon)),
        halo(7, cells.at[3, 4], ret.at[6], (lat, lon_up)),
        halo(8, cells.at[pl.ds(1, 2), 4], ret.at[pl.ds(4, 2)], (lat, lon_up)),
        halo(9, cells.at[4, pl.ds(1, 2)], ret.at[pl.ds(1, 2)], (lat_up, lon)),
    ]

    loads[0].wait()
    loads[1].wait()
    for pair in range(2):
        x = jnp.concatenate([tok[level * 288 + pair * 144 : level * 288 + (pair + 1) * 144, :] for level in range(3)], axis=0)
        y = dot(pin[...], x).astype(BF).reshape(2, 4, CELL, D)
        cells[2 * pair : 2 * pair + 2, 0:4] = y

    pl.semaphore_wait(barrier, len(partners))
    for k in range(4):
        weights[k].start()

    loads[2].wait()
    loads[3].wait()
    at = lax.broadcasted_iota(jnp.int32, (16, 96), 1) - lax.broadcasted_iota(jnp.int32, (16, 96), 0) - (lat * 12 + 3)
    rel = lax.broadcasted_iota(jnp.int32, (16, 96), 0)
    pick_row = jnp.where(((at == 0) | (at == -96)) & (rel < 12), 1.0, 0.0).astype(BF)
    at = lax.broadcasted_iota(jnp.int32, (384, 128), 0) - lax.broadcasted_iota(jnp.int32, (384, 128), 1) - (lon * 24 + 6)
    pick_col = jnp.where((at == 0) | (at == -384), 1.0, 0.0).astype(BF)
    near = dot(dot(pick_row, ids[...].astype(F32).astype(BF)).astype(BF), pick_col)
    near = jnp.where(lax.broadcasted_iota(jnp.int32, (16, 128), 0) == 15, -1.0, near).astype(BF)
    for w in range(4):
        spread = dot(place[w * WIN : (w + 1) * WIN, 0:16], near) * place[w * WIN : (w + 1) * WIN, 128:256].astype(F32)
        column = jnp.sum(spread, axis=1, keepdims=True)
        line = dot_nt(jnp.ones((8, 128), BF), spread.astype(BF))[0:1, :]
        if w == 0:
            bias[0] = jnp.broadcast_to(jnp.where(line < -0.5, NEG, 0.0), (WIN, WIN))
        bias[w + 1] = jnp.where(column == line, 0.0, NEG)

    def step(t, carry):
        @pl.when(t == 0)
        def _():
            for k in range(4, 8):
                loads[k].wait()

        @pl.when(t == 1)
        def _():
            out1[0].start()
            out1[1].start()
            out1[2].start()

        @pl.when(t == 2)
        def _():
            out1[3].start()

        @pl.when(t == 3)
        def _():
            out1[4].start()

        @pl.when(t == 4)
        def _():
            for k in range(8, 12):
                loads[k].wait()
            for k in range(5):
                out1[k].wait()
            weights[0].wait_recv()
            weights[1].wait_recv()
            for k in range(4, 10):
                weights[k].start()

        @pl.when(t == 5)
        def _():
            out2[0].start()
            out2[1].start()
            out2[2].start()

        @pl.when(t == 6)
        def _():
            out2[3].start()

        @pl.when(t == 7)
        def _():
            out2[4].start()
            weights[4].wait_recv()
            weights[5].wait_recv()
            weights[10].start()
            weights[11].start()

        l = t // 4
        u = t - 4 * l
        wr = 1 - u % 2
        wc = 1 - u // 2
        r = l * (1 + 2 * wr) + (1 - l) * 2 * (u // 2)
        c = l * (1 + 2 * wc) + (1 - l) * 2 * (u % 2)
        b = l * (1 + 2 * wr + wc)
        window_block(cells, r, c, l, bias, b, wqkv, wproj, wup, wdown, qkv, att, mid, acc)
        return carry

    lax.fori_loop(0, 8, step, 0)

    for k in range(5):
        out2[k].wait()
    for k in range(4):
        cells[0, k] = ret[k]
    for k in range(3):
        cells[k + 1, 0] = ret[k + 4]

    for k in range(12, 15):
        loads[k].wait()
    for pair in range(2):
        v = dot(pout[...], cells[2 * pair : 2 * pair + 2, 0:4].reshape(8 * CELL, D)).astype(BF)
        for level in range(3):
            fine_s[level * 288 + pair * 144 : level * 288 + (pair + 1) * 144, :] = v[level * 144 : (level + 1) * 144]
    fine_copy = pltpu.make_async_copy(fine_s, fine_o, osem.at[0])
    fine_copy.start()

    every = cells[0:4, 0:4].reshape(16 * CELL, D)
    quad = [dot(quads[k * 256 : (k + 1) * 256, :], every) for k in range(4)]
    normed = layer_norm(jnp.concatenate(quad, axis=1)).astype(BF)
    nq[...] = normed
    merged = dot(nq[...], wm1[...]).astype(BF).astype(F32)
    second = layer_norm(jnp.concatenate([merged[k * 64 : (k + 1) * 64] for k in range(4)], axis=1)).astype(BF)
    rows[0] = second
    weights[12].start()

    loads[15].wait()
    for k in (2, 3, 6, 7, 8, 9, 10, 11):
        weights[k].wait_recv()
    weights[12].wait()

    def columns(j, carry):
        left = jnp.concatenate([rows[0], rows[1]], axis=0)
        right = jnp.concatenate([w2[2 * j], w2[2 * j + 1]], axis=1)
        res = dot(left, right).astype(BF)
        cown[2 * j] = res[0:64, 0:128]
        cown[2 * j + 1] = res[0:64, 128:256]
        cgive[2 * j] = res[64:128, 0:128]
        cgive[2 * j + 1] = res[64:128, 128:256]
        return carry

    lax.fori_loop(0, 4, columns, 0)
    weights[13].start()
    for k in range(8):
        coarse_s[:, pl.ds(pl.multiple_of((2 * k + core) * 128, 128), 128)] = cown[k]
    for k in range(12):
        weights[k].wait_send()
    weights[13].wait()
    for k in range(8):
        coarse_s[:, pl.ds(pl.multiple_of((2 * k + 1 - core) * 128, 128), 128)] = cret[k]
    coarse_copy = pltpu.make_async_copy(coarse_s, coarse_o, osem.at[1])
    coarse_copy.start()
    coarse_copy.wait()
    fine_copy.wait()


def shards(tokens, region_ids, w_qkv, w_proj, w_up, w_down, merge_first, merge_second):
    out_of, quads, place = tables()
    out_of, quads, place = (jnp.asarray(a, BF) for a in (out_of, quads, place))
    vmem = pltpu.VMEM
    fine, coarse = pl.pallas_call(
        kernel,
        out_shape=(jax.ShapeDtypeStruct((864, D), BF), jax.ShapeDtypeStruct((64, 2048), BF)),
        in_specs=[pl.BlockSpec(memory_space=pl.ANY)] * 12,
        out_specs=(pl.BlockSpec(memory_space=pl.ANY),) * 2,
        scratch_shapes=[
            vmem((864, D), BF), vmem((96, 384), jnp.int32), vmem((2, D, 3 * D), BF), vmem((2, D, D), BF),
            vmem((2, D, FF), BF), vmem((2, FF, D), BF), vmem((4 * D, 2 * D), BF), vmem((8, 4096, 128), BF),
            vmem((512, 432), BF), vmem((432, 512), BF), vmem((1024, 1024), BF), vmem((1024, 256), BF),
            vmem((5, 5, CELL, D), BF), vmem((7, CELL, D), BF), vmem((5, WIN, WIN), F32),
            vmem((WIN, 3 * D), BF), vmem((WIN, D), BF), vmem((WIN, D), BF), vmem((WIN, D), F32), vmem((256, 2048), BF),
            vmem((2, 64, 4096), BF), vmem((8, 64, 128), BF), vmem((8, 64, 128), BF), vmem((8, 64, 128), BF),
            vmem((864, D), BF), vmem((64, 2048), BF),
            pltpu.SemaphoreType.DMA((16,)), pltpu.SemaphoreType.DMA((2,)),
            pltpu.SemaphoreType.DMA((10,)), pltpu.SemaphoreType.DMA((10,)),
            pltpu.SemaphoreType.DMA((14,)), pltpu.SemaphoreType.DMA((14,)),
        ],
        compiler_params=pltpu.CompilerParams(
            collective_id=0, has_side_effects=True, vmem_limit_bytes=60 * 1024 * 1024
        ),
    )(
        tokens.reshape(864, D), region_ids, w_qkv, w_proj, w_up, w_down, merge_first, merge_second,
        out_of.T, out_of, quads, place,
    )
    return fine.reshape(3, 12, 24, D), coarse[:54].reshape(3, 3, 6, 2048)


def solution(mesh):
    in_specs = (P(None, "lat", "lon", None), P(), P(), P(), P(), P(), P(), P(None, "lon"))
    out_specs = (P(None, "lat", "lon", None), P(None, "lat", "lon", None))
    return jax.shard_map(shards, mesh=mesh, in_specs=in_specs, out_specs=out_specs, check_vma=False)
```

profile of v0, /device:TPU:25, one launch (start us, length us, event | category | flops | bytes accessed | tf_op | source)
XLA Modules:
  0.0 81.9 jit_solution(13433414625119452543)
XLA Ops:
  0.6 77.4 %shard_map.122 = (bf16[864,512]{1,0:T(8,128)(2,1)}, bf16[64,2048]{1,0:T(8,128)(2,1)}) custom-call(bf16[864,512]{1,0:T(8,128)(2,1)} %bitcast.3, s32[96,384]{1,0:T(8,128)} %ids_h.1, bf16[2,512,1536]{2,1,0:T(8,128)(2,1)} %wqkv_h.1, bf16[2,512,512]{2,1,0:T(8,128)(2,1)} %wproj_h.1, bf16[2,512,2048]{2,1,0:T(8,128)(2,1)} %wup_h.1, bf16[2,2048,512]{2,1,0:T(8,128)(2,1)} %wdown_h.1, ...), custom_call_target="tpu_custom_call" | custom-call | tf_op jit(solution)/shard_map/pallas_call | solution.py:343
  78.1 1.0 %slice.3 = bf16[54,2048]{1,0:T(8,128)(2,1)S(1)} slice(bf16[64,2048]{1,0:T(8,128)(2,1)} %get-tuple-element.5), slice={[0:54], [0:2048]} | slice | bytes 442368 | tf_op jit(solution)/shard_map/slice | solution.py:367
  79.0 0.8 reshape.15
  79.8 2.1 %copy.14 = bf16[3,12,24,512]{3,2,1,0:T(8,128)(2,1)} copy(bf16[3,12,24,512]{3,2,1,0:T(8,128)(2,1)} %bitcast.2) | data formatting | bytes 1769472
where the time goes:
time: 82.1 us; the launch traced here: 81.9 us
  Pallas kernels  77.4 us (94%)
  local copies, waits for them, and re-layouts  3.89 us (5%)
    pallas_call x1, Pallas kernels, shards(): pl.pallas_call(kernel, out_shape=(jax.ShapeDtypeStruct((864, D), BF), jax...  77.4 us
    unnamed x1, local copies, waits for them, and re-layouts  2.15 us

commit v1 on v0

--- a/solution.py
+++ b/solution.py
@@ -19,8 +19,7 @@
 SCORE_SCALE = 0.125 * 1.4426950408889634
 NEG = -1e30
 
-ERF_P = 0.3275911 * 0.7071067811865476
-ERF_A = tuple(0.5 * a for a in (0.254829592, -0.284496736, 1.421413741, -1.453152027, 1.061405429))
+ERF_T = (0.7978281362947702, 0.03646878884975751, -0.00012486010173499664, -3.058133015679481e-05, 1.1191017522607985e-06)
 
 
 def tables():
@@ -73,15 +72,13 @@
 
 
 def gelu(u):
-    size = jnp.abs(u)
-    t = pl.reciprocal(1.0 + ERF_P * size, approx=True)
-    a1, a2, a3, a4, a5 = ERF_A
-    poly = t * (a1 + t * (a2 + t * (a3 + t * (a4 + t * a5))))
-    tail = size * (poly * jnp.exp2(u * u * (-0.5 * 1.4426950408889634)))
-    return jnp.maximum(u, 0.0) - tail
-
-
-def window_block(cells, r, c, l, bias, b, wqkv, wproj, wup, wdown, qkv, att, mid, acc):
+    a = ERF_T
+    w = u * u
+    h = 0.5 * u
+    return h + h * jnp.tanh(u * (a[0] + w * (a[1] + w * (a[2] + w * (a[3] + w * a[4])))))
+
+
+def window_block(cells, r, c, l, bias, b, wqkv, wproj, wup, wdown, qkv, att, mid, acc, nq, between):
     x = cells[pl.ds(r, 2), pl.ds(c, 2)].reshape(WIN, D).astype(F32)
     normed = layer_norm(x).astype(BF)
     for k in range(3):
@@ -106,10 +103,9 @@
     middle = (x + dot(att[...], wproj[l])).astype(BF).astype(F32)
     acc[...] = middle
     mid[...] = layer_norm(middle).astype(BF)
-    for k in range(4):
-        cols = slice(k * 512, (k + 1) * 512)
-        hidden = gelu(dot(mid[...], wup[l, :, cols])).astype(BF)
-        acc[...] += dot(hidden, wdown[l, cols, :])
+    between()
+    nq[...] = gelu(dot(mid[...], wup[l])).astype(BF)
+    acc[...] += dot(nq[...], wdown[l])
     cells[pl.ds(r, 2), pl.ds(c, 2)] = acc[...].astype(BF).reshape(2, 2, CELL, D)
 
 
@@ -117,7 +113,7 @@
     tok_h, ids_h, wqkv_h, wproj_h, wup_h, wdown_h, wm1_h, wm2_h, pin_h, pout_h, quads_h, place_h,
     fine_o, coarse_o,
     tok, ids, wqkv, wproj, wup, wdown, wm1, w2, pin, pout, quads, place,
-    cells, ret, bias, qkv, att, mid, acc, nq, rows, cown, cgive, cret, fine_s, coarse_s,
+    cells, ret, bias, qkv, att, mid, acc, nq, rows, cown, cgive, cret, fine_s, flat, coarse_s,
     lsem, osem, hsend, hrecv, wsend, wrecv,
 ):
     lat, lon = lax.axis_index("lat"), lax.axis_index("lon")
@@ -130,9 +126,14 @@
     side_a = (lat, (1 - xl) * 8 + z * 2 + core)
     side_b = (lax.rem(lat + 4, 8), (1 - xl) * 8 + z * 2 + core)
     twin = (lat, xl * 8 + z * 2 + 1 - core)
+    y = lax.rem(lat, 4)
+    p = lax.rem(y, 2)
+    next_y = lax.rem(y + 1 + 2 * p, 4)
+    other_y = lax.rem(y + 3 - 2 * p, 4)
+    pair1, pair2 = (xh * 4 + next_y, lon), (xh * 4 + other_y, lon)
     partners = (
         (lat_up, lon), (lat_dn, lon), (lat, lon_up), (lat, lon_dn), (lat_up, lon_up), (lat_dn, lon_dn),
-        above, below, side_a, side_b, twin,
+        above, below, side_a, side_b, twin, pair1, pair2,
     )
     barrier = pltpu.get_barrier_semaphore()
     for device in partners:
@@ -146,8 +147,8 @@
         (pout_h, pout), (quads_h, quads), (wm1_h, wm1), (wm2_h, w2.at[mine]),
     ]
     loads = [pltpu.make_async_copy(src, dst, lsem.at[i]) for i, (src, dst) in enumerate(loads)]
-    for load in loads:
-        load.start()
+    for k in range(6):
+        loads[k].start()
 
     def halo(i, src, dst, device):
         return pltpu.make_async_remote_copy(
@@ -159,24 +160,67 @@
             src_ref=src, dst_ref=dst, send_sem=wsend.at[i], recv_sem=wrecv.at[i], device_id=device, device_id_type=MESH
         )
 
-    half = (pl.ds(0, 2048), pl.ds(2048, 2048))
     s_dn, s_up, s_far = xl * 4 + z_dn, xl * 4 + z_up, xl * 4 + z_far
+    o_dn, o_up, o_far = s_dn + 4 - 8 * xl, s_up + 4 - 8 * xl, s_far + 4 - 8 * xl
+
+    def piece(slot, q, count=1):
+        return w2.at[slot, pl.ds(pl.multiple_of(q * 1024, 1024), 1024 * count)]
+
+    def first(q, count=1):
+        return wm2_h.at[pl.ds(pl.multiple_of(q * 1024, 1024), 1024 * count)]
+
+    def pass_on(i, slot, q, device):
+        return give(i, piece(slot, q), piece(slot, q), device)
+
     weights = [
-        give(0, wm2_h, w2.at[mine], above),
-        give(1, wm2_h, w2.at[mine], below),
-        give(2, wm2_h.at[half[0]], w2.at[mine, half[0]], side_a),
-        give(3, wm2_h.at[half[1]], w2.at[mine, half[1]], side_b),
-        give(4, w2.at[s_dn, half[0]], w2.at[s_dn, half[0]], above),
-        give(5, w2.at[s_up, half[1]], w2.at[s_up, half[1]], below),
-        give(6, w2.at[s_dn, half[0]], w2.at[s_dn, half[0]], side_a),
-        give(7, w2.at[s_dn, half[1]], w2.at[s_dn, half[1]], side_b),
-        give(8, w2.at[s_up, half[0]], w2.at[s_up, half[0]], side_a),
-        give(9, w2.at[s_up, half[1]], w2.at[s_up, half[1]], side_b),
-        give(10, w2.at[s_far, half[0]], w2.at[s_far, half[0]], side_a),
-        give(11, w2.at[s_far, half[1]], w2.at[s_far, half[1]], side_b),
-        give(12, rows.at[0], rows.at[1], twin),
-        give(13, cgive, cret, twin),
+        give(0, first(p), piece(mine, p), above),
+        give(1, first(1 - p), piece(mine, 1 - p), above),
+        give(2, first(2 + p), piece(mine, 2 + p), below),
+        give(3, first(3 - p), piece(mine, 3 - p), below),
+        give(4, first(0, 2), piece(mine, 0, 2), side_a),
+        give(5, first(2, 2), piece(mine, 2, 2), side_b),
+        pass_on(6, s_dn, p, above),
+        pass_on(7, s_up, 2 + p, below),
+        pass_on(8, s_dn, p, side_a),
+        pass_on(9, s_up, 2 + p, side_b),
+        give(10, first(2), piece(mine, 2), above),
+        give(11, first(0), piece(mine, 0), below),
+        give(12, first(3), piece(mine, 3), above),
+        give(13, first(1), piece(mine, 1), below),
+        pass_on(14, s_far, p, side_a),
+        pass_on(15, s_far, 2 + p, side_b),
+        pass_on(16, s_far, p, pair1),
+        pass_on(17, s_far, 2 + p, pair1),
+        pass_on(18, o_dn, p, pair2),
+        pass_on(19, o_up, 2 + p, pair2),
+        pass_on(20, s_up, 0, side_a),
+        pass_on(21, s_dn, 2, side_b),
+        pass_on(22, s_up, 1, side_a),
+        pass_on(23, s_dn, 3, side_b),
+        pass_on(24, o_far, p, pair1),
+        pass_on(25, o_far, 2 + p, pair1),
+        give(26, rows.at[0], rows.at[1], twin),
+        give(27, cgive, cret, twin),
     ]
+
+    def stage(received, sent):
+        for k in received:
+            weights[k].wait_recv()
+        for k in sent:
+            weights[k].start()
+
+    stages = {
+        2: ((0, 2), (6, 7, 8, 9)),
+        4: ((), (1, 3)),
+        6: ((6, 7), (16, 17, 14, 15, 10, 11)),
+        8: ((8, 9), (18, 19)),
+        9: ((), (12, 13)),
+        11: ((10, 11), (20, 21)),
+        12: ((14, 15), (24, 25)),
+        14: ((12, 13), (22, 23)),
+    }
+    last = (1, 3, 4, 5, 16, 17, 18, 19, 20, 21, 22, 23, 24, 25)
+
     out1 = [
         halo(0, cells.at[0, 0], cells.at[4, 4], (lat_dn, lon_dn)),
         halo(1, cells.at[0, 1], cells.at[4, 1], (lat_dn, lon)),
@@ -199,8 +243,10 @@
         y = dot(pin[...], x).astype(BF).reshape(2, 4, CELL, D)
         cells[2 * pair : 2 * pair + 2, 0:4] = y
 
+    for k in range(6, 8):
+        loads[k].start()
     pl.semaphore_wait(barrier, len(partners))
-    for k in range(4):
+    for k in (0, 2, 4, 5):
         weights[k].start()
 
     loads[2].wait()
@@ -223,64 +269,69 @@
     def step(t, carry):
         @pl.when(t == 0)
         def _():
-            for k in range(4, 8):
+            for k in range(4, 6):
                 loads[k].wait()
 
         @pl.when(t == 1)
         def _():
-            out1[0].start()
-            out1[1].start()
-            out1[2].start()
+            for k in range(3):
+                out1[k].start()
+            for k in range(8, 16):
+                loads[k].start()
 
         @pl.when(t == 2)
         def _():
+            out1[4].start()
+
+        @pl.when(t == 3)
+        def _():
             out1[3].start()
-
-        @pl.when(t == 3)
-        def _():
-            out1[4].start()
 
         @pl.when(t == 4)
         def _():
             for k in range(8, 12):
                 loads[k].wait()
+
+        @pl.when(t == 5)
+        def _():
             for k in range(5):
                 out1[k].wait()
-            weights[0].wait_recv()
-            weights[1].wait_recv()
-            for k in range(4, 10):
-                weights[k].start()
-
-        @pl.when(t == 5)
-        def _():
-            out2[0].start()
-            out2[1].start()
-            out2[2].start()
 
         @pl.when(t == 6)
         def _():
-            out2[3].start()
+            for k in range(3):
+                out2[k].start()
 
         @pl.when(t == 7)
         def _():
             out2[4].start()
-            weights[4].wait_recv()
-            weights[5].wait_recv()
-            weights[10].start()
-            weights[11].start()
+
+        for at in range(0, 16, 2):
+            if at in stages:
+                pl.when(t == at // 2)(functools.partial(stage, *stages[at]))
+
+        def between():
+            for at in range(1, 16, 2):
+                if at in stages:
+                    pl.when(t == at // 2)(functools.partial(stage, *stages[at]))
+
+            @pl.when(t == 0)
+            def _():
+                for k in range(6, 8):
+                    loads[k].wait()
 
         l = t // 4
         u = t - 4 * l
-        wr = 1 - u % 2
-        wc = 1 - u // 2
-        r = l * (1 + 2 * wr) + (1 - l) * 2 * (u // 2)
-        c = l * (1 + 2 * wc) + (1 - l) * 2 * (u % 2)
-        b = l * (1 + 2 * wr + wc)
-        window_block(cells, r, c, l, bias, b, wqkv, wproj, wup, wdown, qkv, att, mid, acc)
+        odd, high, turn = u % 2, u // 2, ((u + 1) // 2) % 2
+        r = l * (1 + 2 * turn) + (1 - l) * 2 * odd
+        c = l * (1 + 2 * odd) + (1 - l) * 2 * high
+        b = l * (1 + 2 * turn + odd)
+        window_block(cells, r, c, l, bias, b, wqkv, wproj, wup, wdown, qkv, att, mid, acc, nq, between)
         return carry
 
     lax.fori_loop(0, 8, step, 0)
 
+    out2[3].start()
     for k in range(5):
         out2[k].wait()
     for k in range(4):
@@ -304,12 +355,12 @@
     merged = dot(nq[...], wm1[...]).astype(BF).astype(F32)
     second = layer_norm(jnp.concatenate([merged[k * 64 : (k + 1) * 64] for k in range(4)], axis=1)).astype(BF)
     rows[0] = second
-    weights[12].start()
+    weights[26].start()
 
     loads[15].wait()
-    for k in (2, 3, 6, 7, 8, 9, 10, 11):
+    for k in last:
         weights[k].wait_recv()
-    weights[12].wait()
+    weights[26].wait()
 
     def columns(j, carry):
         left = jnp.concatenate([rows[0], rows[1]], axis=0)
@@ -322,14 +373,16 @@
         return carry
 
     lax.fori_loop(0, 4, columns, 0)
-    weights[13].start()
+    weights[27].start()
     for k in range(8):
-        coarse_s[:, pl.ds(pl.multiple_of((2 * k + core) * 128, 128), 128)] = cown[k]
-    for k in range(12):
+        flat[:, pl.ds(pl.multiple_of((2 * k + core) * 128, 128), 128)] = cown[k].astype(F32)
+    for k in range(26):
         weights[k].wait_send()
-    weights[13].wait()
+    weights[27].wait()
     for k in range(8):
-        coarse_s[:, pl.ds(pl.multiple_of((2 * k + 1 - core) * 128, 128), 128)] = cret[k]
+        flat[:, pl.ds(pl.multiple_of((2 * k + 1 - core) * 128, 128), 128)] = cret[k].astype(F32)
+    for k in range(9):
+        coarse_s[k // 3, k % 3] = flat[6 * k : 6 * k + 6, :].astype(BF)
     coarse_copy = pltpu.make_async_copy(coarse_s, coarse_o, osem.at[1])
     coarse_copy.start()
     coarse_copy.wait()
@@ -342,7 +395,7 @@
     vmem = pltpu.VMEM
     fine, coarse = pl.pallas_call(
         kernel,
-        out_shape=(jax.ShapeDtypeStruct((864, D), BF), jax.ShapeDtypeStruct((64, 2048), BF)),
+        out_shape=(jax.ShapeDtypeStruct((864, D), BF), jax.ShapeDtypeStruct((3, 3, 6, 2048), BF)),
         in_specs=[pl.BlockSpec(memory_space=pl.ANY)] * 12,
         out_specs=(pl.BlockSpec(memory_space=pl.ANY),) * 2,
         scratch_shapes=[
@@ -352,10 +405,10 @@
             vmem((5, 5, CELL, D), BF), vmem((7, CELL, D), BF), vmem((5, WIN, WIN), F32),
             vmem((WIN, 3 * D), BF), vmem((WIN, D), BF), vmem((WIN, D), BF), vmem((WIN, D), F32), vmem((256, 2048), BF),
             vmem((2, 64, 4096), BF), vmem((8, 64, 128), BF), vmem((8, 64, 128), BF), vmem((8, 64, 128), BF),
-            vmem((864, D), BF), vmem((64, 2048), BF),
+            vmem((864, D), BF), vmem((64, 2048), F32), vmem((3, 3, 6, 2048), BF),
             pltpu.SemaphoreType.DMA((16,)), pltpu.SemaphoreType.DMA((2,)),
             pltpu.SemaphoreType.DMA((10,)), pltpu.SemaphoreType.DMA((10,)),
-            pltpu.SemaphoreType.DMA((14,)), pltpu.SemaphoreType.DMA((14,)),
+            pltpu.SemaphoreType.DMA((28,)), pltpu.SemaphoreType.DMA((28,)),
         ],
         compiler_params=pltpu.CompilerParams(
             collective_id=0, has_side_effects=True, vmem_limit_bytes=60 * 1024 * 1024
@@ -364,7 +417,7 @@
         tokens.reshape(864, D), region_ids, w_qkv, w_proj, w_up, w_down, merge_first, merge_second,
         out_of.T, out_of, quads, place,
     )
-    return fine.reshape(3, 12, 24, D), coarse[:54].reshape(3, 3, 6, 2048)
+    return fine.reshape(3, 12, 24, D), coarse
 
 
 def solution(mesh):

time: 82.1 us -> 70.7 us (0.86)
  the two profiles are of different devices: /device:TPU:25 before, /device:TPU:1 now
where the time goes in v1:
time: 70.7 us; the launch traced here: 69.4 us
  Pallas kernels  64.9 us (92%)
  local copies, waits for them, and re-layouts  3.84 us (5%)
    pallas_call x1, Pallas kernels, shards(): pl.pallas_call(kernel, out_shape=(jax.ShapeDtypeStruct((864, D), BF), jax...  64.9 us
    unnamed x2, local copies, waits for them, and re-layouts  3.84 us

profile of v1, /device:TPU:1, one launch (start us, length us, event | category | flops | bytes accessed | tf_op | source)
XLA Modules:
  0.0 69.4 jit_solution(4333047390237050329)
XLA Ops:
  0.6 64.9 %shard_map.122 = (bf16[864,512]{1,0:T(8,128)(2,1)}, bf16[3,3,6,2048]{3,2,1,0:T(8,128)(2,1)}) custom-call(bf16[864,512]{1,0:T(8,128)(2,1)} %bitcast.3, s32[96,384]{1,0:T(8,128)} %ids_h.1, bf16[2,512,1536]{2,1,0:T(8,128)(2,1)} %wqkv_h.1, bf16[2,512,512]{2,1,0:T(8,128)(2,1)} %wproj_h.1, bf16[2,512,2048]{2,1,0:T(8,128)(2,1)} %wup_h.1, ...), custom_call_target="tpu_custom_call" | custom-call | tf_op jit(solution)/shard_map/pallas_call | solution.py:396
  65.6 2.1 %copy.15 = bf16[3,12,24,512]{3,2,1,0:T(8,128)(2,1)} copy(bf16[3,12,24,512]{3,2,1,0:T(8,128)(2,1)} %bitcast.2) | data formatting | bytes 1769472
  67.7 1.7 %copy.16 = bf16[3,3,6,2048]{3,2,1,0:T(8,128)(2,1)} copy(bf16[3,3,6,2048]{3,2,1,0:T(8,128)(2,1)} %get-tuple-element.9) | data formatting | bytes 442368

commit v2 on v1

--- a/solution.py
+++ b/solution.py
@@ -19,7 +19,7 @@
 SCORE_SCALE = 0.125 * 1.4426950408889634
 NEG = -1e30
 
-ERF_T = (0.7978281362947702, 0.03646878884975751, -0.00012486010173499664, -3.058133015679481e-05, 1.1191017522607985e-06)
+ERF_T = (0.7975078650001068, 0.03700566160227986, -0.00035151904076978317)
 
 
 def tables():
@@ -72,10 +72,11 @@
 
 
 def gelu(u):
-    a = ERF_T
-    w = u * u
-    h = 0.5 * u
-    return h + h * jnp.tanh(u * (a[0] + w * (a[1] + w * (a[2] + w * (a[3] + w * a[4])))))
+    u = u.astype(BF)
+    a0, a1, a2 = (jnp.asarray(v, BF) for v in ERF_T)
+    w = jnp.minimum(u * u, jnp.asarray(26.0, BF))
+    h = jnp.asarray(0.5, BF) * u
+    return h + h * jnp.tanh(u * (a0 + w * (a1 + w * a2)))
 
 
 def window_block(cells, r, c, l, bias, b, wqkv, wproj, wup, wdown, qkv, att, mid, acc, nq, between):
@@ -113,7 +114,7 @@
     tok_h, ids_h, wqkv_h, wproj_h, wup_h, wdown_h, wm1_h, wm2_h, pin_h, pout_h, quads_h, place_h,
     fine_o, coarse_o,
     tok, ids, wqkv, wproj, wup, wdown, wm1, w2, pin, pout, quads, place,
-    cells, ret, bias, qkv, att, mid, acc, nq, rows, cown, cgive, cret, fine_s, flat, coarse_s,
+    cells, ret, bias, qkv, att, mid, acc, nq, rows, away, cown, cgive, cret, fgive, fret, fine_s, flat, coarse_s,
     lsem, osem, hsend, hrecv, wsend, wrecv,
 ):
     lat, lon = lax.axis_index("lat"), lax.axis_index("lon")
@@ -125,26 +126,26 @@
     above, below = (lat, xl * 8 + z_up * 2 + core), (lat, xl * 8 + z_dn * 2 + core)
     side_a = (lat, (1 - xl) * 8 + z * 2 + core)
     side_b = (lax.rem(lat + 4, 8), (1 - xl) * 8 + z * 2 + core)
+    side_a2 = (lat, (1 - xl) * 8 + z * 2 + 1 - core)
+    side_b2 = (lax.rem(lat + 4, 8), (1 - xl) * 8 + z * 2 + 1 - core)
     twin = (lat, xl * 8 + z * 2 + 1 - core)
     y = lax.rem(lat, 4)
     p = lax.rem(y, 2)
     next_y = lax.rem(y + 1 + 2 * p, 4)
-    other_y = lax.rem(y + 3 - 2 * p, 4)
-    pair1, pair2 = (xh * 4 + next_y, lon), (xh * 4 + other_y, lon)
+    pair = (xh * 4 + next_y, lon)
     partners = (
         (lat_up, lon), (lat_dn, lon), (lat, lon_up), (lat, lon_dn), (lat_up, lon_up), (lat_dn, lon_dn),
-        above, below, side_a, side_b, twin, pair1, pair2,
+        above, below, side_a, side_b, twin, pair, side_a2, side_b2,
     )
     barrier = pltpu.get_barrier_semaphore()
     for device in partners:
         pl.semaphore_signal(barrier, inc=1, device_id=device, device_id_type=MESH)
 
-    mine = xl * 4 + z
     loads = [
         (tok_h, tok), (pin_h, pin), (ids_h, ids), (place_h, place),
         (wqkv_h.at[0], wqkv.at[0]), (wproj_h.at[0], wproj.at[0]), (wup_h.at[0], wup.at[0]), (wdown_h.at[0], wdown.at[0]),
         (wqkv_h.at[1], wqkv.at[1]), (wproj_h.at[1], wproj.at[1]), (wup_h.at[1], wup.at[1]), (wdown_h.at[1], wdown.at[1]),
-        (pout_h, pout), (quads_h, quads), (wm1_h, wm1), (wm2_h, w2.at[mine]),
+        (pout_h, pout), (quads_h, quads), (wm1_h, wm1), (wm2_h, w2.at[z]),
     ]
     loads = [pltpu.make_async_copy(src, dst, lsem.at[i]) for i, (src, dst) in enumerate(loads)]
     for k in range(6):
@@ -160,9 +161,6 @@
             src_ref=src, dst_ref=dst, send_sem=wsend.at[i], recv_sem=wrecv.at[i], device_id=device, device_id_type=MESH
         )
 
-    s_dn, s_up, s_far = xl * 4 + z_dn, xl * 4 + z_up, xl * 4 + z_far
-    o_dn, o_up, o_far = s_dn + 4 - 8 * xl, s_up + 4 - 8 * xl, s_far + 4 - 8 * xl
-
     def piece(slot, q, count=1):
         return w2.at[slot, pl.ds(pl.multiple_of(q * 1024, 1024), 1024 * count)]
 
@@ -173,35 +171,27 @@
         return give(i, piece(slot, q), piece(slot, q), device)
 
     weights = [
-        give(0, first(p), piece(mine, p), above),
-        give(1, first(1 - p), piece(mine, 1 - p), above),
-        give(2, first(2 + p), piece(mine, 2 + p), below),
-        give(3, first(3 - p), piece(mine, 3 - p), below),
-        give(4, first(0, 2), piece(mine, 0, 2), side_a),
-        give(5, first(2, 2), piece(mine, 2, 2), side_b),
-        pass_on(6, s_dn, p, above),
-        pass_on(7, s_up, 2 + p, below),
-        pass_on(8, s_dn, p, side_a),
-        pass_on(9, s_up, 2 + p, side_b),
-        give(10, first(2), piece(mine, 2), above),
-        give(11, first(0), piece(mine, 0), below),
-        give(12, first(3), piece(mine, 3), above),
-        give(13, first(1), piece(mine, 1), below),
-        pass_on(14, s_far, p, side_a),
-        pass_on(15, s_far, 2 + p, side_b),
-        pass_on(16, s_far, p, pair1),
-        pass_on(17, s_far, 2 + p, pair1),
-        pass_on(18, o_dn, p, pair2),
-        pass_on(19, o_up, 2 + p, pair2),
-        pass_on(20, s_up, 0, side_a),
-        pass_on(21, s_dn, 2, side_b),
-        pass_on(22, s_up, 1, side_a),
-        pass_on(23, s_dn, 3, side_b),
-        pass_on(24, o_far, p, pair1),
-        pass_on(25, o_far, 2 + p, pair1),
-        give(26, rows.at[0], rows.at[1], twin),
-        give(27, cgive, cret, twin),
+        give(0, first(p), piece(z, p), above),
+        give(1, first(1 - p), piece(z, 1 - p), above),
+        give(2, first(2 + p), piece(z, 2 + p), below),
+        give(3, first(3 - p), piece(z, 3 - p), below),
+        pass_on(4, z_dn, p, above),
+        pass_on(5, z_up, 2 + p, below),
+        pass_on(6, z_far, p, pair),
+        pass_on(7, z_far, 2 + p, pair),
+        give(8, first(2), piece(z, 2), above),
+        give(9, first(0), piece(z, 0), below),
+        give(10, first(3), piece(z, 3), above),
+        give(11, first(1), piece(z, 1), below),
     ]
+    to_twin = give(12, rows.at[0], rows.at[1], twin)
+    from_twin = give(13, cgive, cret, twin)
+    across = [
+        give(14, rows.at[0, pl.ds(0, 32)], away.at[0], side_a),
+        give(15, rows.at[0, pl.ds(32, 32)], away.at[1], side_b),
+    ]
+    around = [give(16 + k, away.at[k], away.at[2 + k], twin) for k in range(2)]
+    back = [give(18 + k, fgive.at[k], fret.at[k], device) for k, device in enumerate((side_a, side_b, side_a2, side_b2))]
 
     def stage(received, sent):
         for k in received:
@@ -210,16 +200,12 @@
             weights[k].start()
 
     stages = {
-        2: ((0, 2), (6, 7, 8, 9)),
-        4: ((), (1, 3)),
-        6: ((6, 7), (16, 17, 14, 15, 10, 11)),
-        8: ((8, 9), (18, 19)),
-        9: ((), (12, 13)),
-        11: ((10, 11), (20, 21)),
-        12: ((14, 15), (24, 25)),
-        14: ((12, 13), (22, 23)),
+        3: ((0, 2), (4, 5)),
+        5: ((), (1, 3)),
+        8: ((4, 5), (6, 7, 8, 9)),
+        11: ((), (10, 11)),
     }
-    last = (1, 3, 4, 5, 16, 17, 18, 19, 20, 21, 22, 23, 24, 25)
+    last = (1, 3, 6, 7, 8, 9, 10, 11)
 
     out1 = [
         halo(0, cells.at[0, 0], cells.at[4, 4], (lat_dn, lon_dn)),
@@ -246,7 +232,7 @@
     for k in range(6, 8):
         loads[k].start()
     pl.semaphore_wait(barrier, len(partners))
-    for k in (0, 2, 4, 5):
+    for k in (0, 2):
         weights[k].start()
 
     loads[2].wait()
@@ -341,12 +327,6 @@
 
     for k in range(12, 15):
         loads[k].wait()
-    for pair in range(2):
-        v = dot(pout[...], cells[2 * pair : 2 * pair + 2, 0:4].reshape(8 * CELL, D)).astype(BF)
-        for level in range(3):
-            fine_s[level * 288 + pair * 144 : level * 288 + (pair + 1) * 144, :] = v[level * 144 : (level + 1) * 144]
-    fine_copy = pltpu.make_async_copy(fine_s, fine_o, osem.at[0])
-    fine_copy.start()
 
     every = cells[0:4, 0:4].reshape(16 * CELL, D)
     quad = [dot(quads[k * 256 : (k + 1) * 256, :], every) for k in range(4)]
@@ -355,38 +335,81 @@
     merged = dot(nq[...], wm1[...]).astype(BF).astype(F32)
     second = layer_norm(jnp.concatenate([merged[k * 64 : (k + 1) * 64] for k in range(4)], axis=1)).astype(BF)
     rows[0] = second
-    weights[26].start()
+    across[0].start()
+    across[1].start()
+    to_twin.start()
+
+    for pair in range(2):
+        v = dot(pout[...], cells[2 * pair : 2 * pair + 2, 0:4].reshape(8 * CELL, D)).astype(BF)
+        for level in range(3):
+            fine_s[level * 288 + pair * 144 : level * 288 + (pair + 1) * 144, :] = v[level * 144 : (level + 1) * 144]
+    fine_copy = pltpu.make_async_copy(fine_s, fine_o, osem.at[0])
+    fine_copy.start()
 
     loads[15].wait()
     for k in last:
         weights[k].wait_recv()
-    weights[26].wait()
-
-    def columns(j, carry):
+    to_twin.wait()
+
+    def near_columns(j, carry):
         left = jnp.concatenate([rows[0], rows[1]], axis=0)
-        right = jnp.concatenate([w2[2 * j], w2[2 * j + 1]], axis=1)
-        res = dot(left, right).astype(BF)
+        res = dot(left, jnp.concatenate([w2[2 * j], w2[2 * j + 1]], axis=1)).astype(BF)
         cown[2 * j] = res[0:64, 0:128]
         cown[2 * j + 1] = res[0:64, 128:256]
         cgive[2 * j] = res[64:128, 0:128]
         cgive[2 * j + 1] = res[64:128, 128:256]
         return carry
 
-    lax.fori_loop(0, 4, columns, 0)
-    weights[27].start()
-    for k in range(8):
-        flat[:, pl.ds(pl.multiple_of((2 * k + core) * 128, 128), 128)] = cown[k].astype(F32)
-    for k in range(26):
+    lax.fori_loop(0, 2, near_columns, 0)
+    from_twin.start()
+    for k in range(2):
+        across[k].wait_recv()
+        around[k].start()
+    for k in range(2):
+        around[k].wait_recv()
+
+    def far_columns(j, carry):
+        left = away[...].reshape(128, 4096)
+        res = dot(left, jnp.concatenate([w2[2 * j], w2[2 * j + 1]], axis=1)).astype(BF)
+        for k in range(4):
+            fgive[k, 2 * j] = res[32 * k : 32 * k + 32, 0:128]
+            fgive[k, 2 * j + 1] = res[32 * k : 32 * k + 32, 128:256]
+        return carry
+
+    lax.fori_loop(0, 2, far_columns, 0)
+    for copy in back:
+        copy.start()
+
+    def block(side, k, c):
+        return pl.ds(pl.multiple_of((side * 8 + 2 * k + c) * 128, 128), 128)
+
+    for k in range(12):
         weights[k].wait_send()
-    weights[27].wait()
-    for k in range(8):
-        flat[:, pl.ds(pl.multiple_of((2 * k + 1 - core) * 128, 128), 128)] = cret[k].astype(F32)
+    for k in range(2):
+        across[k].wait_send()
+        around[k].wait_send()
+    from_twin.wait()
+    for k in range(4):
+        flat[:, block(xl, k, core)] = cown[k].astype(F32)
+        flat[:, block(xl, k, 1 - core)] = cret[k].astype(F32)
+    for copy in back:
+        copy.wait()
+    for k in range(4):
+        flat[0:32, block(1 - xl, k, core)] = fret[0, k].astype(F32)
+        flat[32:64, block(1 - xl, k, core)] = fret[1, k].astype(F32)
+        flat[0:32, block(1 - xl, k, 1 - core)] = fret[2, k].astype(F32)
+        flat[32:64, block(1 - xl, k, 1 - core)] = fret[3, k].astype(F32)
     for k in range(9):
         coarse_s[k // 3, k % 3] = flat[6 * k : 6 * k + 6, :].astype(BF)
     coarse_copy = pltpu.make_async_copy(coarse_s, coarse_o, osem.at[1])
     coarse_copy.start()
     coarse_copy.wait()
     fine_copy.wait()
+
+
+def hand_over(fine_i, coarse_i, fine_o, coarse_o):
+    fine_o[...] = fine_i[...]
+    coarse_o[...] = coarse_i[...]
 
 
 def shards(tokens, region_ids, w_qkv, w_proj, w_up, w_down, merge_first, merge_second):
@@ -400,15 +423,16 @@
         out_specs=(pl.BlockSpec(memory_space=pl.ANY),) * 2,
         scratch_shapes=[
             vmem((864, D), BF), vmem((96, 384), jnp.int32), vmem((2, D, 3 * D), BF), vmem((2, D, D), BF),
-            vmem((2, D, FF), BF), vmem((2, FF, D), BF), vmem((4 * D, 2 * D), BF), vmem((8, 4096, 128), BF),
+            vmem((2, D, FF), BF), vmem((2, FF, D), BF), vmem((4 * D, 2 * D), BF), vmem((4, 4096, 128), BF),
             vmem((512, 432), BF), vmem((432, 512), BF), vmem((1024, 1024), BF), vmem((1024, 256), BF),
             vmem((5, 5, CELL, D), BF), vmem((7, CELL, D), BF), vmem((5, WIN, WIN), F32),
             vmem((WIN, 3 * D), BF), vmem((WIN, D), BF), vmem((WIN, D), BF), vmem((WIN, D), F32), vmem((256, 2048), BF),
-            vmem((2, 64, 4096), BF), vmem((8, 64, 128), BF), vmem((8, 64, 128), BF), vmem((8, 64, 128), BF),
+            vmem((2, 64, 4096), BF), vmem((4, 32, 4096), BF), vmem((4, 64, 128), BF), vmem((4, 64, 128), BF), vmem((4, 64, 128), BF),
+            vmem((4, 4, 32, 128), BF), vmem((4, 4, 32, 128), BF),
             vmem((864, D), BF), vmem((64, 2048), F32), vmem((3, 3, 6, 2048), BF),
             pltpu.SemaphoreType.DMA((16,)), pltpu.SemaphoreType.DMA((2,)),
             pltpu.SemaphoreType.DMA((10,)), pltpu.SemaphoreType.DMA((10,)),
-            pltpu.SemaphoreType.DMA((28,)), pltpu.SemaphoreType.DMA((28,)),
+            pltpu.SemaphoreType.DMA((22,)), pltpu.SemaphoreType.DMA((22,)),
         ],
         compiler_params=pltpu.CompilerParams(
             collective_id=0, has_side_effects=True, vmem_limit_bytes=60 * 1024 * 1024
@@ -417,6 +441,14 @@
         tokens.reshape(864, D), region_ids, w_qkv, w_proj, w_up, w_down, merge_first, merge_second,
         out_of.T, out_of, quads, place,
     )
+    specs = (pl.BlockSpec((288, D), lambda k: (k, 0)), pl.BlockSpec((1, 3, 6, 2048), lambda k: (k, 0, 0, 0)))
+    fine, coarse = pl.pallas_call(
+        hand_over,
+        grid=(3,),
+        out_shape=(jax.ShapeDtypeStruct(fine.shape, BF), jax.ShapeDtypeStruct(coarse.shape, BF)),
+        in_specs=list(specs),
+        out_specs=specs,
+    )(fine, coarse)
     return fine.reshape(3, 12, 24, D), coarse
 
 

time: 70.7 us -> 64.8 us (0.917); the launches traced: 69.4 us -> 64.6 us
  local copies, waits for them, and re-layouts: 3.84 us -> 0 us
  Pallas kernels: 64.9 us -> 64 us
    pallas_call x1, Pallas kernels: 64.9 us -> 60.9 us  [shards(): pl.pallas_call(kernel, out_shape=(jax.ShapeDtypeStruct((864, D), BF), jax...]
    unnamed x2 -> x0, local copies, waits for them, and re-layouts: 3.84 us -> none
    pallas_call x0 -> x1, Pallas kernels: none -> 3.09 us  [shards(): pl.pallas_call(hand_over, grid=(3,), out_shape=(jax.ShapeDtypeStruct(fine...]
where the time goes in v2:
time: 64.8 us; the launch traced here: 64.6 us
  Pallas kernels  64 us (99%)
    pallas_call x1, Pallas kernels, shards(): pl.pallas_call(kernel, out_shape=(jax.ShapeDtypeStruct((864, D), BF), jax...  60.9 us
    pallas_call x1, Pallas kernels, shards(): pl.pallas_call(hand_over, grid=(3,), out_shape=(jax.ShapeDtypeStruct(fine...  3.09 us

profile of v2, /device:TPU:1, one launch (start us, length us, event | category | flops | bytes accessed | tf_op | source)
XLA Modules:
  0.0 64.6 jit_solution(8308614631063950065)
XLA Ops:
  0.6 60.9 %shard_map.122 = (bf16[864,512]{1,0:T(8,128)(2,1)}, bf16[3,3,6,2048]{3,2,1,0:T(8,128)(2,1)}) custom-call(bf16[864,512]{1,0:T(8,128)(2,1)} %bitcast.2, s32[96,384]{1,0:T(8,128)} %ids_h.1, bf16[2,512,1536]{2,1,0:T(8,128)(2,1)} %wqkv_h.1, bf16[2,512,512]{2,1,0:T(8,128)(2,1)} %wproj_h.1, bf16[2,512,2048]{2,1,0:T(8,128)(2,1)} %wup_h.1, ...), custom_call_target="tpu_custom_call" | custom-call | tf_op jit(solution)/shard_map/pallas_call | solution.py:419
  61.5 3.1 %shard_map.123 = (bf16[864,512]{1,0:T(8,128)(2,1)}, bf16[3,3,6,2048]{3,2,1,0:T(8,128)(2,1)}) custom-call(bf16[864,512]{1,0:T(8,128)(2,1)} %get-tuple-element.6.fine_i, bf16[3,3,6,2048]{3,2,1,0:T(8,128)(2,1)} %get-tuple-element.7.coarse_i), custom_call_target="tpu_custom_call" | custom-call | tf_op jit(solution)/shard_map/pallas_call | solution.py:445

commit v3 on v2

--- a/solution.py
+++ b/solution.py
@@ -187,10 +187,17 @@
     to_twin = give(12, rows.at[0], rows.at[1], twin)
     from_twin = give(13, cgive, cret, twin)
     across = [
-        give(14, rows.at[0, pl.ds(0, 32)], away.at[0], side_a),
-        give(15, rows.at[0, pl.ds(32, 32)], away.at[1], side_b),
-    ]
-    around = [give(16 + k, away.at[k], away.at[2 + k], twin) for k in range(2)]
+        give(14, rows.at[0, pl.ds(0, 16)], away.at[0, pl.ds(0, 16)], side_a),
+        give(15, rows.at[0, pl.ds(32, 16)], away.at[1, pl.ds(0, 16)], side_b),
+        give(22, rows.at[0, pl.ds(16, 16)], away.at[0, pl.ds(16, 16)], side_a),
+        give(23, rows.at[0, pl.ds(48, 16)], away.at[1, pl.ds(16, 16)], side_b),
+    ]
+    around = [
+        give(16, away.at[0, pl.ds(0, 16)], away.at[2, pl.ds(0, 16)], twin),
+        give(17, away.at[1, pl.ds(0, 16)], away.at[3, pl.ds(0, 16)], twin),
+        give(24, away.at[0, pl.ds(16, 16)], away.at[2, pl.ds(16, 16)], twin),
+        give(25, away.at[1, pl.ds(16, 16)], away.at[3, pl.ds(16, 16)], twin),
+    ]
     back = [give(18 + k, fgive.at[k], fret.at[k], device) for k, device in enumerate((side_a, side_b, side_a2, side_b2))]
 
     def stage(received, sent):
@@ -200,10 +207,9 @@
             weights[k].start()
 
     stages = {
-        3: ((0, 2), (4, 5)),
-        5: ((), (1, 3)),
-        8: ((4, 5), (6, 7, 8, 9)),
-        11: ((), (10, 11)),
+        4: ((0, 2), (4, 5, 1, 3)),
+        8: ((4, 5), (6, 7)),
+        10: ((), (8, 9, 10, 11)),
     }
     last = (1, 3, 6, 7, 8, 9, 10, 11)
 
@@ -335,9 +341,9 @@
     merged = dot(nq[...], wm1[...]).astype(BF).astype(F32)
     second = layer_norm(jnp.concatenate([merged[k * 64 : (k + 1) * 64] for k in range(4)], axis=1)).astype(BF)
     rows[0] = second
-    across[0].start()
-    across[1].start()
     to_twin.start()
+    for copy in across:
+        copy.start()
 
     for pair in range(2):
         v = dot(pout[...], cells[2 * pair : 2 * pair + 2, 0:4].reshape(8 * CELL, D)).astype(BF)
@@ -362,10 +368,10 @@
 
     lax.fori_loop(0, 2, near_columns, 0)
     from_twin.start()
-    for k in range(2):
+    for k in range(4):
         across[k].wait_recv()
         around[k].start()
-    for k in range(2):
+    for k in range(4):
         around[k].wait_recv()
 
     def far_columns(j, carry):
@@ -385,7 +391,7 @@
 
     for k in range(12):
         weights[k].wait_send()
-    for k in range(2):
+    for k in range(4):
         across[k].wait_send()
         around[k].wait_send()
     from_twin.wait()
@@ -432,7 +438,7 @@
             vmem((864, D), BF), vmem((64, 2048), F32), vmem((3, 3, 6, 2048), BF),
             pltpu.SemaphoreType.DMA((16,)), pltpu.SemaphoreType.DMA((2,)),
             pltpu.SemaphoreType.DMA((10,)), pltpu.SemaphoreType.DMA((10,)),
-            pltpu.SemaphoreType.DMA((22,)), pltpu.SemaphoreType.DMA((22,)),
+            pltpu.SemaphoreType.DMA((26,)), pltpu.SemaphoreType.DMA((26,)),
         ],
         compiler_params=pltpu.CompilerParams(
             collective_id=0, has_side_effects=True, vmem_limit_bytes=60 * 1024 * 1024

time: 64.8 us -> 64.7 us (level)
  no operation moved by 1% of the time
where the time goes in v3:
time: 64.7 us; the launch traced here: 64.6 us
  Pallas kernels  63.9 us (99%)
    pallas_call x1, Pallas kernels, shards(): pl.pallas_call(kernel, out_shape=(jax.ShapeDtypeStruct((864, D), BF), jax...  60.8 us
    pallas_call x1, Pallas kernels, shards(): pl.pallas_call(hand_over, grid=(3,), out_shape=(jax.ShapeDtypeStruct(fine...  3.09 us

profile of v3, /device:TPU:1, one launch (start us, length us, event | category | flops | bytes accessed | tf_op | source)
XLA Modules:
  0.0 64.6 jit_solution(5774081746535781400)
XLA Ops:
  0.6 60.8 %shard_map.122 = (bf16[864,512]{1,0:T(8,128)(2,1)}, bf16[3,3,6,2048]{3,2,1,0:T(8,128)(2,1)}) custom-call(bf16[864,512]{1,0:T(8,128)(2,1)} %bitcast.2, s32[96,384]{1,0:T(8,128)} %ids_h.1, bf16[2,512,1536]{2,1,0:T(8,128)(2,1)} %wqkv_h.1, bf16[2,512,512]{2,1,0:T(8,128)(2,1)} %wproj_h.1, bf16[2,512,2048]{2,1,0:T(8,128)(2,1)} %wup_h.1, ...), custom_call_target="tpu_custom_call" | custom-call | tf_op jit(solution)/shard_map/pallas_call | solution.py:425
  61.5 3.1 %shard_map.123 = (bf16[864,512]{1,0:T(8,128)(2,1)}, bf16[3,3,6,2048]{3,2,1,0:T(8,128)(2,1)}) custom-call(bf16[864,512]{1,0:T(8,128)(2,1)} %get-tuple-element.6.fine_i, bf16[3,3,6,2048]{3,2,1,0:T(8,128)(2,1)} %get-tuple-element.7.coarse_i), custom_call_target="tpu_custom_call" | custom-call | tf_op jit(solution)/shard_map/pallas_call | solution.py:451
